TPU v7x, 32 devices: a whole 2x2x4 slice. The times are simulated.
32 devices in a mesh: row: 8 (over y, x, core), col: 4 (over z).
Axes of the slice: x: 2, y: 2, z: 4, core: 2. Of those that a mesh axis runs over, the one named last changes fastest.
Arguments:
- record: bfloat16 [6, 2048, 2560], P(None, ('row', 'col')), may hold values from -6 to 6
- taps: float32 [200], replicated, may hold values from -0.4375 to 0.4375
- plan: int32 [6], replicated, may hold values from 0 to 5, each once
- quality: int32 [2048], P(('row', 'col')), may hold values 0 or 1
Outputs:
- correlation: float32 [51, 2048, 2048], P(None, 'row', 'col')
Inputs may be any that keep to these rules, and one draw needn't show every extreme that they name: plan is a permutation of the recorded sub-windows; its first 4 entries name the ones that are stacked.
All inputs are finite; a program needn't handle non-finite values. No bound on the sum of `quality` on one device may be relied on, other than what follows from the above.
Results may differ from a plain program's by a relative error of at most 0.0039.
Values may be sent and summed in bfloat16 or wider, within the bound.
A program may use at most 128 MiB of HBM per device.

v0:
```python
import functools
import math

import jax
import jax.numpy as jnp
from jax import lax
from jax.experimental import pallas as pl
from jax.experimental.pallas import tpu as pltpu
from jax.sharding import PartitionSpec as P

STRIDE = 20
TAPS = 200
HALFWIN = 32
MAXLAG = 25
SUB = 4
LAGS = 51
LANES = 128
BAND_FRAMES = 32
BAND_STEP = BAND_FRAMES * STRIDE
BAND_WIDTH = 896
PARTS = 3
LAG_GROUP = 3
SLOTS = 3

MESH = pl.DeviceIdType.MESH
NT = (((1,), (1,)), ((), ()))


def split_parts(values, count):
    parts = []
    for _ in range(count):
        part = values.astype(jnp.bfloat16)
        parts.append(part)
        values = values - part.astype(jnp.float32)
    return parts


def filter_band(tap_row):
    base = jnp.broadcast_to(tap_row, (8, TAPS))
    base = jnp.concatenate([base, jnp.zeros((8, BAND_WIDTH - TAPS), jnp.float32)], axis=1)
    place = lax.broadcasted_iota(jnp.int32, (8, BAND_WIDTH), 0)
    groups = []
    for group in range(BAND_FRAMES // 8):
        held = jnp.zeros((8, BAND_WIDTH), jnp.float32)
        for row in range(8):
            shift = (group * 8 + row) * STRIDE
            moved = base if shift == 0 else pltpu.roll(base, shift, 1)
            held = jnp.where(place == row, moved, held)
        groups.append(held)
    return jnp.concatenate(groups, axis=0)


def nearest_first(cols):
    return [sorted(range(cols), key=lambda other: (abs(other - c), other)) for c in range(cols)]


def whiten_and_send(
    rows, cols, plan_hbm, tap_hbm, quality_hbm, record_ref,
    source_ref, receiver_ref,
    raw, table, plan_ref, tap_ref, quality_ref,
    load_sem, source_sem, receiver_sem, out_sem, plane_sem, twin_sem,
):
    r, c = lax.axis_index("row"), lax.axis_index("col")
    parity = lax.rem(r, 2)
    pair = lax.div(r, 2)
    twin = r + 1 - 2 * parity
    on_diagonal = pair == c
    slots, chans, length = raw.shape
    frames = length // STRIDE
    bits = cols.bit_length() - 1

    loads = [
        pltpu.make_async_copy(tap_hbm, tap_ref, load_sem.at[slots]),
        pltpu.make_async_copy(plan_hbm, plan_ref, load_sem.at[slots + 1]),
        pltpu.make_async_copy(quality_hbm, quality_ref, load_sem.at[slots + 2]),
    ] + [pltpu.make_async_copy(record_ref.at[i], raw.at[i], load_sem.at[i]) for i in range(slots)]
    for load in loads:
        load.start()

    def bit(value, k):
        return lax.rem(lax.div(value, 2**k), 2)

    def across(k):
        return r + 2 * 2**k * (1 - 2 * bit(pair, k))

    barrier = pltpu.get_barrier_semaphore()

    def greet(row, col):
        pl.semaphore_signal(barrier, inc=1, device_id=(row, col), device_id_type=MESH)

    for step in range(1, cols):
        greet(r, lax.rem(c + step, cols))
    for k in range(bits):
        greet(across(k), c)
    greet(twin, c)

    table[...] = jnp.zeros_like(table)
    loads[0].wait()
    band = filter_band(tap_ref[...])
    for number, part in enumerate(split_parts(band, PARTS)):
        for block in range(frames // BAND_FRAMES):
            start = block * BAND_STEP
            width = min(BAND_WIDTH, length - start)
            first = number * frames + block * BAND_FRAMES
            table[first : first + BAND_FRAMES, start : start + width] = part[:, :width]

    for load in loads[1:]:
        load.wait()
    picked = jnp.concatenate([raw[plan_ref[s]] for s in range(SUB)], axis=0)
    summed = lax.dot_general(picked, table[...], NT, preferred_element_type=jnp.float32)
    decimated = summed[:, :frames]
    for number in range(1, PARTS):
        decimated = decimated + summed[:, number * frames : (number + 1) * frames]

    near = lax.broadcasted_iota(jnp.int32, (frames, frames), 0)
    near = jnp.abs(near - lax.broadcasted_iota(jnp.int32, (frames, frames), 1)) <= HALFWIN
    near = near.astype(jnp.float32).astype(jnp.bfloat16)
    envelope = jnp.zeros_like(decimated)
    for part in split_parts(jnp.abs(decimated), PARTS):
        envelope = envelope + jnp.dot(part, near, preferred_element_type=jnp.float32)
    envelope = envelope / (2 * HALFWIN + 1)
    square = lax.broadcasted_iota(jnp.int32, (chans, chans), 0) == lax.broadcasted_iota(
        jnp.int32, (chans, chans), 1
    )
    usable = jnp.broadcast_to(quality_ref[...].astype(jnp.float32), (chans, chans))
    usable = jnp.sum(jnp.where(square, usable, 0.0), axis=1, keepdims=True)
    scaled = decimated / (envelope + 1e-05)
    for s in range(SUB):
        window = scaled[s * chans : (s + 1) * chans] * usable
        source_ref[c, :, s * frames : (s + 1) * frames] = window.astype(jnp.bfloat16)

    pl.semaphore_wait(barrier, cols - 1 + bits + 1)

    def remote(src, dst, send_sem, recv_sem, row, col):
        return pltpu.make_async_remote_copy(
            src_ref=src, dst_ref=dst, send_sem=send_sem, recv_sem=recv_sem,
            device_id=(row, col), device_id_type=MESH,
        )

    def along(step):
        target = lax.rem(pair + step, cols)
        copy = remote(
            source_ref.at[c], source_ref.at[c], out_sem.at[step], source_sem.at[c], r, target
        )
        return target != c, copy

    for step in range(cols):
        other, copy = along(step)
        pl.when(other)(copy.start)

    def source_arrival(number):
        return remote(
            source_ref.at[number], source_ref.at[number], out_sem.at[0], source_sem.at[number],
            r, lax.rem(c + 1, cols),
        )

    half = parity * cols

    def receiver_arrival(number):
        return remote(
            receiver_ref.at[number], receiver_ref.at[number], out_sem.at[0],
            receiver_sem.at[number], twin, c,
        )

    def hand_on(block, number, to, send_sem):
        return remote(
            block, receiver_ref.at[half + number], send_sem, receiver_sem.at[half + number], to, c
        )

    order = nearest_first(cols)

    def place(step):
        number = jnp.int32(order[0][step])
        for column in range(1, cols):
            number = jnp.where(c == column, order[column][step], number)
        return number

    differs = [bit(pair, k) != bit(c, k) for k in range(bits)]

    def passes_on(step, k):
        ahead = range(k + 1) if step % 2 == 0 else range(k, bits)
        free = jnp.logical_not(differs[k])
        for other in ahead:
            free = jnp.logical_and(free, jnp.logical_not(differs[other]))
        return free

    def kept(step):
        number = place(step)
        return pltpu.make_async_copy(
            source_ref.at[number], receiver_ref.at[half + number], load_sem.at[step]
        )

    @pl.when(on_diagonal)
    def _():
        for step in range(cols):
            number = place(step)
            if step > 0:
                source_arrival(number).wait_recv()
            for k in range(bits):
                hand_on(source_ref.at[number], number, across(k), plane_sem.at[step, k]).start()
            hand_on(source_ref.at[number], number, twin, twin_sem.at[step]).start()
            kept(step).start()
        for step in range(cols):
            kept(step).wait()

    @pl.when(jnp.logical_not(on_diagonal))
    def _():
        for step in range(cols):
            number = place(step)
            mine = receiver_ref.at[half + number]
            receiver_arrival(half + number).wait_recv()
            for k in range(bits):
                pl.when(passes_on(step, k))(
                    hand_on(mine, number, across(k), plane_sem.at[step, k]).start
                )
            hand_on(mine, number, twin, twin_sem.at[step]).start()
        for step in range(1, cols):
            source_arrival(lax.rem(c + step, cols)).wait_recv()

    for number in range(cols):
        receiver_arrival(cols - half + number).wait_recv()
    for step in range(cols):
        other, copy = along(step)
        pl.when(other)(copy.wait_send)
        block = receiver_ref.at[half + step]
        for k in range(bits):
            sent = jnp.logical_or(on_diagonal, passes_on(step, k))
            pl.when(sent)(hand_on(block, step, across(k), plane_sem.at[step, k]).wait_send)
        hand_on(block, step, twin, twin_sem.at[step]).wait_send()


def correlate(scale, source_ref, receiver_ref, out_ref, wide, turned, held, sems):
    frames = LANES
    width = source_ref.shape[1]
    windows = width // frames
    groups = out_ref.shape[0] // LAG_GROUP
    wide[...] = source_ref[...].astype(jnp.float32)
    turned[...] = receiver_ref[...].astype(jnp.float32).T.astype(jnp.bfloat16)
    lane = lax.broadcasted_iota(jnp.int32, (source_ref.shape[0], frames), 1)

    def send(group):
        slot = lax.rem(group, SLOTS)
        return pltpu.make_async_copy(
            held.at[slot], out_ref.at[pl.ds(group * LAG_GROUP, LAG_GROUP)], sems.at[slot]
        )

    def step(group, carry):
        slot = lax.rem(group, SLOTS)

        @pl.when(group >= SLOTS)
        def _():
            send(group - SLOTS).wait()

        for inner in range(LAG_GROUP):
            lag = group * LAG_GROUP + inner - MAXLAG
            from_place = lane - lag
            inside = jnp.logical_and(from_place >= 0, from_place < frames)
            shift = lax.rem(lag + frames, frames)
            moved = [
                jnp.where(
                    inside, pltpu.roll(wide[:, s * frames : (s + 1) * frames], shift, 1), 0.0
                ).astype(jnp.bfloat16)
                for s in range(windows)
            ]
            moved = jnp.concatenate(moved, axis=1)
            product = jnp.dot(moved, turned[...], preferred_element_type=jnp.float32)
            held[slot, inner] = product * scale
        send(group).start()
        return carry

    lax.fori_loop(0, groups, step, 0)
    for group in range(groups - SLOTS, groups):
        send(group).wait()


def body(rows, cols, record, taps, plan, quality):
    slots, chans, length = record.shape
    width = SUB * (length // STRIDE)
    hbm = pl.BlockSpec(memory_space=pltpu.HBM)
    vmem = pl.BlockSpec(memory_space=pltpu.VMEM)
    anywhere = pl.BlockSpec(memory_space=pl.ANY)
    operands = (plan, taps.reshape(1, TAPS), quality.reshape(1, chans), record)
    source, receiver = pl.pallas_call(
        functools.partial(whiten_and_send, rows, cols),
        out_shape=(
            jax.ShapeDtypeStruct((cols, chans, width), jnp.bfloat16),
            jax.ShapeDtypeStruct((2 * cols, chans, width), jnp.bfloat16),
        ),
        in_specs=[hbm] * 4,
        out_specs=(vmem, vmem),
        scratch_shapes=[
            pltpu.VMEM((slots, chans, length), jnp.bfloat16),
            pltpu.VMEM((PARTS * (length // STRIDE), length), jnp.bfloat16),
            pltpu.SMEM(plan.shape, jnp.int32),
            pltpu.VMEM((1, TAPS), jnp.float32),
            pltpu.VMEM((1, chans), jnp.int32),
            pltpu.SemaphoreType.DMA((max(slots + 3, cols),)),
            pltpu.SemaphoreType.DMA((cols,)),
            pltpu.SemaphoreType.DMA((2 * cols,)),
            pltpu.SemaphoreType.DMA((cols,)),
            pltpu.SemaphoreType.DMA((cols, cols.bit_length() - 1)),
            pltpu.SemaphoreType.DMA((cols,)),
        ],
        compiler_params=pltpu.CompilerParams(
            collective_id=0, has_side_effects=True, vmem_limit_bytes=32 * 2**20
        ),
        name="whiten_and_send",
    )(*(pltpu.with_memory_space_constraint(held, pltpu.HBM) for held in operands))
    sources = cols * chans
    receivers = 2 * cols * chans
    return pl.pallas_call(
        functools.partial(correlate, 1.0 / math.sqrt(width)),
        out_shape=jax.ShapeDtypeStruct((LAGS, sources, receivers), jnp.float32),
        in_specs=[vmem, vmem],
        out_specs=anywhere,
        scratch_shapes=[
            pltpu.VMEM((sources, width), jnp.float32),
            pltpu.VMEM((width, receivers), jnp.bfloat16),
            pltpu.VMEM((SLOTS, LAG_GROUP, sources, receivers), jnp.float32),
            pltpu.SemaphoreType.DMA((SLOTS,)),
        ],
        compiler_params=pltpu.CompilerParams(vmem_limit_bytes=32 * 2**20),
        cost_estimate=pl.CostEstimate(
            flops=2 * LAGS * sources * receivers * width,
            bytes_accessed=4 * LAGS * sources * receivers,
            transcendentals=0,
        ),
        name="correlate",
    )(source.reshape(sources, width), receiver.reshape(receivers, width))


def solution(mesh):
    rows, cols = mesh.shape["row"], mesh.shape["col"]
    in_specs = (P(None, ("row", "col"), None), P(), P(), P(("row", "col")))
    out_specs = P(None, "row", "col")
    return jax.shard_map(
        functools.partial(body, rows, cols),
        mesh=mesh,
        in_specs=in_specs,
        out_specs=out_specs,
        check_vma=False,
    )
```

profile of v0, /device:TPU:25, one launch (start us, length us, event | category | flops | bytes accessed | tf_op | source)
XLA Modules:
  0.0 32.0 jit_solution(5596852587236670177)
XLA Ops:
  0.0 19.9 %whiten_and_send.1 = (bf16[4,64,512]{2,1,0:T(8,128)(2,1)S(1)}, bf16[8,64,512]{2,1,0:T(8,128)(2,1)S(1)}) custom-call(s32[6]{0:T(128)} %plan_hbm.1, f32[1,200]{1,0:T(1,128)} %bitcast.6, s32[1,64]{1,0:T(1,128)} %bitcast.7, bf16[6,64,2560]{2,1,0:T(8,128)(2,1)} %record_ref.1), custom_call_target="tpu_custom_call" | custom-call | tf_op jit(solution)/shard_map/whiten_and_send/pallas_call | solution.py:283
  19.9 12.1 %correlate.1 = f32[51,256,512]{2,1,0:T(8,128)} custom-call(bf16[256,512]{1,0:T(8,128)(2,1)S(1)} %bitcast.5, bf16[512,512]{1,0:T(8,128)(2,1)S(1)} %bitcast.4), custom_call_target="tpu_custom_call" | custom-call | flops 6845104128 | bytes 26738688 | tf_op jit(solution)/shard_map/correlate/pallas_call | solution.py:311
where the time goes:
time: 32.2 us; the launch traced here: 32 us
  Pallas kernels  32 us (99%)
    pallas_call x1, Pallas kernels, body(): pl.pallas_call(functools.partial(whiten_and_send, rows, cols), out_shape=...  19.9 us
    pallas_call x1, Pallas kernels, body(): pl.pallas_call(functools.partial(correlate, 1.0 / math.sqrt(width)), out_...  12.1 us

commit v1 on v0

--- a/solution.py
+++ b/solution.py
@@ -229,14 +229,14 @@
         hand_on(block, step, twin, twin_sem.at[step]).wait_send()
 
 
-def correlate(scale, source_ref, receiver_ref, out_ref, wide, turned, held, sems):
+def correlate(scale, source_ref, receiver_ref, out_ref, wide, turned, even, odd, held, sems):
     frames = LANES
-    width = source_ref.shape[1]
+    sources, width = source_ref.shape
     windows = width // frames
     groups = out_ref.shape[0] // LAG_GROUP
-    wide[...] = source_ref[...].astype(jnp.float32)
+    wide[...] = source_ref[...]
     turned[...] = receiver_ref[...].astype(jnp.float32).T.astype(jnp.bfloat16)
-    lane = lax.broadcasted_iota(jnp.int32, (source_ref.shape[0], frames), 1)
+    lane = lax.broadcasted_iota(jnp.int32, (sources, frames), 1)
 
     def send(group):
         slot = lax.rem(group, SLOTS)
@@ -244,7 +244,26 @@
             held.at[slot], out_ref.at[pl.ds(group * LAG_GROUP, LAG_GROUP)], sems.at[slot]
         )
 
-    def step(group, carry):
+    def fill(moved, group, inner):
+        lag = group * LAG_GROUP + inner - MAXLAG
+        from_place = lane - lag
+        inside = jnp.logical_and(from_place >= 0, from_place < frames)
+        shift = lax.rem(lag + frames, frames)
+        for s in range(windows):
+            window = pltpu.roll(wide[:, s * frames : (s + 1) * frames], shift, 1)
+            moved[inner * sources : (inner + 1) * sources, s * frames : (s + 1) * frames] = (
+                jnp.where(inside, window, 0.0).astype(jnp.bfloat16)
+            )
+
+    def multiply(moved, slot, inner):
+        product = jnp.dot(
+            moved[inner * sources : (inner + 1) * sources, :],
+            turned[...],
+            preferred_element_type=jnp.float32,
+        )
+        held[slot, inner] = product * scale
+
+    def turn(group, now, later):
         slot = lax.rem(group, SLOTS)
 
         @pl.when(group >= SLOTS)
@@ -252,23 +271,21 @@
             send(group - SLOTS).wait()
 
         for inner in range(LAG_GROUP):
-            lag = group * LAG_GROUP + inner - MAXLAG
-            from_place = lane - lag
-            inside = jnp.logical_and(from_place >= 0, from_place < frames)
-            shift = lax.rem(lag + frames, frames)
-            moved = [
-                jnp.where(
-                    inside, pltpu.roll(wide[:, s * frames : (s + 1) * frames], shift, 1), 0.0
-                ).astype(jnp.bfloat16)
-                for s in range(windows)
-            ]
-            moved = jnp.concatenate(moved, axis=1)
-            product = jnp.dot(moved, turned[...], preferred_element_type=jnp.float32)
-            held[slot, inner] = product * scale
+            multiply(now, slot, inner)
+            if later is not None:
+                fill(later, group + 1, inner)
         send(group).start()
+
+    for inner in range(LAG_GROUP):
+        fill(even, 0, inner)
+
+    def step(index, carry):
+        turn(2 * index, even, odd)
+        turn(2 * index + 1, odd, even)
         return carry
 
-    lax.fori_loop(0, groups, step, 0)
+    lax.fori_loop(0, groups // 2, step, 0)
+    turn(groups - 1, even, None)
     for group in range(groups - SLOTS, groups):
         send(group).wait()
 
@@ -314,8 +331,10 @@
         in_specs=[vmem, vmem],
         out_specs=anywhere,
         scratch_shapes=[
-            pltpu.VMEM((sources, width), jnp.float32),
+            pltpu.VMEM((sources, width), jnp.bfloat16),
             pltpu.VMEM((width, receivers), jnp.bfloat16),
+            pltpu.VMEM((LAG_GROUP * sources, width), jnp.bfloat16),
+            pltpu.VMEM((LAG_GROUP * sources, width), jnp.bfloat16),
             pltpu.VMEM((SLOTS, LAG_GROUP, sources, receivers), jnp.float32),
             pltpu.SemaphoreType.DMA((SLOTS,)),
         ],

time: 32.2 us -> 31.6 us (0.981)
  Pallas kernels: 32 us -> 31.4 us
    pallas_call x1, Pallas kernels: 12.1 us -> 11.5 us  [body(): pl.pallas_call(functools.partial(correlate, 1.0 / math.sqrt(width)), out_...]
where the time goes in v1:
time: 31.6 us; the launch traced here: 31.4 us
  Pallas kernels  31.4 us (99%)
    pallas_call x1, Pallas kernels, body(): pl.pallas_call(functools.partial(whiten_and_send, rows, cols), out_shape=...  19.9 us
    pallas_call x1, Pallas kernels, body(): pl.pallas_call(functools.partial(correlate, 1.0 / math.sqrt(width)), out_...  11.5 us

profile of v1, /device:TPU:25, one launch (start us, length us, event | category | flops | bytes accessed | tf_op | source)
XLA Modules:
  0.0 31.4 jit_solution(4097959191068742173)
XLA Ops:
  0.0 19.9 %whiten_and_send.1 = (bf16[4,64,512]{2,1,0:T(8,128)(2,1)S(1)}, bf16[8,64,512]{2,1,0:T(8,128)(2,1)S(1)}) custom-call(s32[6]{0:T(128)} %plan_hbm.1, f32[1,200]{1,0:T(1,128)} %bitcast.6, s32[1,64]{1,0:T(1,128)} %bitcast.7, bf16[6,64,2560]{2,1,0:T(8,128)(2,1)} %record_ref.1), custom_call_target="tpu_custom_call" | custom-call | tf_op jit(solution)/shard_map/whiten_and_send/pallas_call | solution.py:300
  19.9 11.5 %correlate.1 = f32[51,256,512]{2,1,0:T(8,128)} custom-call(bf16[256,512]{1,0:T(8,128)(2,1)S(1)} %bitcast.5, bf16[512,512]{1,0:T(8,128)(2,1)S(1)} %bitcast.4), custom_call_target="tpu_custom_call" | custom-call | flops 6845104128 | bytes 26738688 | tf_op jit(solution)/shard_map/correlate/pallas_call | solution.py:328
